TPU v7x, 256 devices: a whole 4x4x8 slice. The times are simulated.
256 devices in a mesh: grp: 8 (over y, core), dev: 32 (over x, z).
Axes of the slice: x: 4, y: 4, z: 8, core: 2. Of those that a mesh axis runs over, the one named last changes fastest.
Arguments:
- features: bfloat16 [512, 128, 768], P(('grp', 'dev'))
- tile_counts: int32 [512], P(('grp', 'dev')), may hold values from 20 to 120
- projection: bfloat16 [768, 512], replicated, may hold values from -0.21875 to 0.21875
Outputs:
- tile_maxima: float32 [512, 512, 128], P('grp', 'dev')
- chamfer: float32 [512, 512], P('grp', 'dev')
All inputs are finite; a program needn't handle non-finite values.
Results may differ from a plain program's by a relative error of at most 0.0014.
Values may be sent and summed in bfloat16 or wider, within the bound.
A program may use at most 64 MiB of HBM per device.

v0:
```python
import math

import jax
import jax.numpy as jnp
from jax import lax
from jax.sharding import PartitionSpec as P


def spread(value, axis, root):
    mine = lax.axis_index(axis) == root
    return lax.psum(jnp.where(mine, value, jnp.zeros_like(value)), axis)


def embed_tiles(features, projection):
    raw = jnp.einsum("spf,fe->spe", features, projection, preferred_element_type=jnp.float32)
    scale = lax.rsqrt(jnp.sum(raw * raw, axis=2, keepdims=True) + 1e-06)
    return (raw * scale).astype(jnp.bfloat16)


def score_block(rows, row_counts, cols, col_counts):
    slots = rows.shape[1]
    position = jnp.arange(slots, dtype=jnp.int32)
    row_valid = position[None, :] < row_counts[:, None]
    col_valid = position[None, :] < col_counts[:, None]
    score = jnp.einsum("ape,bqe->abpq", rows, cols, preferred_element_type=jnp.float32)
    forward = jnp.max(jnp.where(col_valid[None, :, None, :], score, -4.0), axis=3)
    forward = jnp.where(row_valid[:, None, :], forward, 0.0)
    back = jnp.max(jnp.where(row_valid[:, None, :, None], score, -4.0), axis=2)
    back = jnp.where(col_valid[None, :, :], back, 0.0)
    row_mean = jnp.sum(forward, axis=2) / row_counts[:, None].astype(jnp.float32)
    col_mean = jnp.sum(back, axis=2) / col_counts[None, :].astype(jnp.float32)
    return (forward, 0.5 * (row_mean + col_mean))


def on_device(features, tile_counts, projection):
    ratio = lax.axis_size("dev") // lax.axis_size("grp")
    column = lax.axis_index("dev")
    holder = column // ratio
    own = embed_tiles(features, projection)
    rows, row_counts = (
        lax.all_gather(own, "dev", axis=0, tiled=True),
        lax.all_gather(tile_counts, "dev", axis=0, tiled=True),
    )
    width = rows.shape[0] // ratio
    offset = column % ratio * width
    piece = lax.dynamic_slice_in_dim(rows, offset, width, 0)
    piece_counts = lax.dynamic_slice_in_dim(row_counts, offset, width, 0)
    cols, col_counts = (spread(piece, "grp", holder), spread(piece_counts, "grp", holder))
    total = rows.shape[0]
    group = math.gcd(total, 4)
    blocks = rows.reshape(total // group, group, rows.shape[1], rows.shape[2])
    block_counts = row_counts.reshape(total // group, group)

    def one_block(pair):
        return score_block(pair[0], pair[1], cols, col_counts)

    forward, chamfer = lax.map(one_block, (blocks, block_counts))
    tile_maxima = forward.reshape(total, cols.shape[0], rows.shape[1])
    return (tile_maxima, chamfer.reshape(total, cols.shape[0]))


def solution(mesh):
    return jax.shard_map(
        on_device,
        mesh=mesh,
        in_specs=(P(("grp", "dev"), None, None), P(("grp", "dev")), P()),
        out_specs=(P("grp", "dev", None), P("grp", "dev")),
        check_vma=False,
    )
```

profile of v0, /device:TPU:5, one launch (start us, length us, event | category | flops | bytes accessed | tf_op | source)
XLA Modules:
  0.0 257.7 jit_solution(18070428982514950656)
XLA Ops:
  7.2 1.1 copy-done
  8.3 1.4 multiply_reduce_fusion
  10.7 99.8 %all-gather.2.cloned.1.call-done = bf16[64,128,512]{2,1,0:T(8,128)(2,1)} async-done(((bf16[2,128,512]{2,1,0:T(8,128)(2,1)}), bf16[64,128,512]{2,1,0:T(8,128)(2,1)}) %all-gather.2.cloned.1.call-update) | async-done | bytes 8388624 | tf_op jit(solution)/shard_map/all_gather | solution.py:41
  110.5 3.0 %dynamic-slice_select_fusion = bf16[16,128,512]{2,1,0:T(8,128)(2,1)} fusion(bf16[64,128,512]{2,1,0:T(8,128)(2,1)} %all-gather.2.cloned.1.call-done, s32[]{:T(128)S(6)} %select_n.66, pred[]{:T(512)S(6)} %eq.6), kind=kLoop, calls=%fused_computation.18 | loop fusion | flops 1048576 | bytes 4194309 | tf_op jit(solution)/shard_map/jit(_where)/select_n | solution.py:11
  115.1 13.3 %all-reduce = s32[64]{0:T(128)S(1)} all-reduce(s32[64]{0:T(128)S(1)} %dynamic-update-slice), channel_id=1, replica_groups=mesh['grp'=8,'dev'=32] {'dev'}, use_global_device_ids=true, to_apply=%add | all-reduce | flops 64 | bytes 512
  128.5 12.5 %psum.14 = s32[16]{0:T(128)S(1)} all-reduce(s32[16]{0:T(128)S(1)} %broadcast_select_fusion), channel_id=1, replica_groups=mesh['grp'=8,'dev'=32] {'grp'}, use_global_device_ids=true, to_apply=%region_1.2 | all-reduce | flops 16 | bytes 128 | tf_op jit(solution)/shard_map/psum | solution.py:11
  141.0 40.7 %all-reduce.3.cloned.1.call-done = bf16[16,128,512]{2,1,0:T(8,128)(2,1)} async-done(((bf16[16,128,512]{2,1,0:T(8,128)(2,1)}), bf16[16,128,512]{2,1,0:T(8,128)(2,1)}) %all-reduce.3.cloned.1.call-update) | async-done | bytes 2097168 | tf_op jit(solution)/shard_map/psum | solution.py:11
  181.7 68.4 %while.13 = (s32[]{:T(128)}, f32[16,4,16,128]{3,2,1,0:T(8,128)}, f32[16,4,16]{2,1,0:T(4,128)S(1)}, s32[16,4]{1,0:T(8,128)S(1)}, s32[16]{0:T(128)S(1)}, /*index=5...) while((s32[]{:T(128)}, f32[16,4,16,128]{3,2,1,0:T(8,128)}, ...), condition=%wide.region_8.9_spmd, body=%wide.region_3.8_spmd.sunk | while | flops 1077963392 | bytes 2835173 | solution.py:57
  181.9 3.3 %select_reduce_fusion.4 = (f32[4,16,128]{2,1,0:T(8,128)S(1)}, f32[4,128,16]{1,2,0:T(8,128)S(1)}) fusion(pred[4,128]{1,0:T(4,128)(4,1)S(1)} %iota_compare_fusion.4, pred[16,128]{1,0:T(8,128)(4,1)S(1)} %iota_compare_fusion.5, bf16[16,128,512]{2,1,0:T(8,128)(2,1)} %get-tuple-element.188, bf16[16,4,128,512]{3,2,1,0:T(8,128)(2,1)} %get-tuple-element.187, ...), kind=kOutput, calls=%fused_computation.clone.1 | convolution fusion | flops 1077919744 | bytes 2690048 | tf_op jit(solution)/shard_map/while/body/eval_jaxpr/ape,bqe->abpq/dot_general | solution.py:25
  186.2 3.3 %select_reduce_fusion.4 = (f32[4,16,128]{2,1,0:T(8,128)S(1)}, f32[4,128,16]{1,2,0:T(8,128)S(1)}) fusion(pred[4,128]{1,0:T(4,128)(4,1)S(1)} %iota_compare_fusion.4, pred[16,128]{1,0:T(8,128)(4,1)S(1)} %iota_compare_fusion.5, bf16[16,128,512]{2,1,0:T(8,128)(2,1)} %get-tuple-element.188, bf16[16,4,128,512]{3,2,1,0:T(8,128)(2,1)} %get-tuple-element.187, ...), kind=kOutput, calls=%fused_computation.clone.1 | convolution fusion | flops 1077919744 | bytes 2690048 | tf_op jit(solution)/shard_map/while/body/eval_jaxpr/ape,bqe->abpq/dot_general | solution.py:25
  190.4 3.3 %select_reduce_fusion.4 = (f32[4,16,128]{2,1,0:T(8,128)S(1)}, f32[4,128,16]{1,2,0:T(8,128)S(1)}) fusion(pred[4,128]{1,0:T(4,128)(4,1)S(1)} %iota_compare_fusion.4, pred[16,128]{1,0:T(8,128)(4,1)S(1)} %iota_compare_fusion.5, bf16[16,128,512]{2,1,0:T(8,128)(2,1)} %get-tuple-element.188, bf16[16,4,128,512]{3,2,1,0:T(8,128)(2,1)} %get-tuple-element.187, ...), kind=kOutput, calls=%fused_computation.clone.1 | convolution fusion | flops 1077919744 | bytes 2690048 | tf_op jit(solution)/shard_map/while/body/eval_jaxpr/ape,bqe->abpq/dot_general | solution.py:25
  194.7 3.3 %select_reduce_fusion.4 = (f32[4,16,128]{2,1,0:T(8,128)S(1)}, f32[4,128,16]{1,2,0:T(8,128)S(1)}) fusion(pred[4,128]{1,0:T(4,128)(4,1)S(1)} %iota_compare_fusion.4, pred[16,128]{1,0:T(8,128)(4,1)S(1)} %iota_compare_fusion.5, bf16[16,128,512]{2,1,0:T(8,128)(2,1)} %get-tuple-element.188, bf16[16,4,128,512]{3,2,1,0:T(8,128)(2,1)} %get-tuple-element.187, ...), kind=kOutput, calls=%fused_computation.clone.1 | convolution fusion | flops 1077919744 | bytes 2690048 | tf_op jit(solution)/shard_map/while/body/eval_jaxpr/ape,bqe->abpq/dot_general | solution.py:25
  199.0 3.3 %select_reduce_fusion.4 = (f32[4,16,128]{2,1,0:T(8,128)S(1)}, f32[4,128,16]{1,2,0:T(8,128)S(1)}) fusion(pred[4,128]{1,0:T(4,128)(4,1)S(1)} %iota_compare_fusion.4, pred[16,128]{1,0:T(8,128)(4,1)S(1)} %iota_compare_fusion.5, bf16[16,128,512]{2,1,0:T(8,128)(2,1)} %get-tuple-element.188, bf16[16,4,128,512]{3,2,1,0:T(8,128)(2,1)} %get-tuple-element.187, ...), kind=kOutput, calls=%fused_computation.clone.1 | convolution fusion | flops 1077919744 | bytes 2690048 | tf_op jit(solution)/shard_map/while/body/eval_jaxpr/ape,bqe->abpq/dot_general | solution.py:25
  203.3 3.3 %select_reduce_fusion.4 = (f32[4,16,128]{2,1,0:T(8,128)S(1)}, f32[4,128,16]{1,2,0:T(8,128)S(1)}) fusion(pred[4,128]{1,0:T(4,128)(4,1)S(1)} %iota_compare_fusion.4, pred[16,128]{1,0:T(8,128)(4,1)S(1)} %iota_compare_fusion.5, bf16[16,128,512]{2,1,0:T(8,128)(2,1)} %get-tuple-element.188, bf16[16,4,128,512]{3,2,1,0:T(8,128)(2,1)} %get-tuple-element.187, ...), kind=kOutput, calls=%fused_computation.clone.1 | convolution fusion | flops 1077919744 | bytes 2690048 | tf_op jit(solution)/shard_map/while/body/eval_jaxpr/ape,bqe->abpq/dot_general | solution.py:25
  207.5 3.3 %select_reduce_fusion.4 = (f32[4,16,128]{2,1,0:T(8,128)S(1)}, f32[4,128,16]{1,2,0:T(8,128)S(1)}) fusion(pred[4,128]{1,0:T(4,128)(4,1)S(1)} %iota_compare_fusion.4, pred[16,128]{1,0:T(8,128)(4,1)S(1)} %iota_compare_fusion.5, bf16[16,128,512]{2,1,0:T(8,128)(2,1)} %get-tuple-element.188, bf16[16,4,128,512]{3,2,1,0:T(8,128)(2,1)} %get-tuple-element.187, ...), kind=kOutput, calls=%fused_computation.clone.1 | convolution fusion | flops 1077919744 | bytes 2690048 | tf_op jit(solution)/shard_map/while/body/eval_jaxpr/ape,bqe->abpq/dot_general | solution.py:25
  211.8 3.3 %select_reduce_fusion.4 = (f32[4,16,128]{2,1,0:T(8,128)S(1)}, f32[4,128,16]{1,2,0:T(8,128)S(1)}) fusion(pred[4,128]{1,0:T(4,128)(4,1)S(1)} %iota_compare_fusion.4, pred[16,128]{1,0:T(8,128)(4,1)S(1)} %iota_compare_fusion.5, bf16[16,128,512]{2,1,0:T(8,128)(2,1)} %get-tuple-element.188, bf16[16,4,128,512]{3,2,1,0:T(8,128)(2,1)} %get-tuple-element.187, ...), kind=kOutput, calls=%fused_computation.clone.1 | convolution fusion | flops 1077919744 | bytes 2690048 | tf_op jit(solution)/shard_map/while/body/eval_jaxpr/ape,bqe->abpq/dot_general | solution.py:25
  216.1 3.3 %select_reduce_fusion.4 = (f32[4,16,128]{2,1,0:T(8,128)S(1)}, f32[4,128,16]{1,2,0:T(8,128)S(1)}) fusion(pred[4,128]{1,0:T(4,128)(4,1)S(1)} %iota_compare_fusion.4, pred[16,128]{1,0:T(8,128)(4,1)S(1)} %iota_compare_fusion.5, bf16[16,128,512]{2,1,0:T(8,128)(2,1)} %get-tuple-element.188, bf16[16,4,128,512]{3,2,1,0:T(8,128)(2,1)} %get-tuple-element.187, ...), kind=kOutput, calls=%fused_computation.clone.1 | convolution fusion | flops 1077919744 | bytes 2690048 | tf_op jit(solution)/shard_map/while/body/eval_jaxpr/ape,bqe->abpq/dot_general | solution.py:25
  220.4 3.3 %select_reduce_fusion.4 = (f32[4,16,128]{2,1,0:T(8,128)S(1)}, f32[4,128,16]{1,2,0:T(8,128)S(1)}) fusion(pred[4,128]{1,0:T(4,128)(4,1)S(1)} %iota_compare_fusion.4, pred[16,128]{1,0:T(8,128)(4,1)S(1)} %iota_compare_fusion.5, bf16[16,128,512]{2,1,0:T(8,128)(2,1)} %get-tuple-element.188, bf16[16,4,128,512]{3,2,1,0:T(8,128)(2,1)} %get-tuple-element.187, ...), kind=kOutput, calls=%fused_computation.clone.1 | convolution fusion | flops 1077919744 | bytes 2690048 | tf_op jit(solution)/shard_map/while/body/eval_jaxpr/ape,bqe->abpq/dot_general | solution.py:25
  224.7 3.3 %select_reduce_fusion.4 = (f32[4,16,128]{2,1,0:T(8,128)S(1)}, f32[4,128,16]{1,2,0:T(8,128)S(1)}) fusion(pred[4,128]{1,0:T(4,128)(4,1)S(1)} %iota_compare_fusion.4, pred[16,128]{1,0:T(8,128)(4,1)S(1)} %iota_compare_fusion.5, bf16[16,128,512]{2,1,0:T(8,128)(2,1)} %get-tuple-element.188, bf16[16,4,128,512]{3,2,1,0:T(8,128)(2,1)} %get-tuple-element.187, ...), kind=kOutput, calls=%fused_computation.clone.1 | convolution fusion | flops 1077919744 | bytes 2690048 | tf_op jit(solution)/shard_map/while/body/eval_jaxpr/ape,bqe->abpq/dot_general | solution.py:25
  228.9 3.3 %select_reduce_fusion.4 = (f32[4,16,128]{2,1,0:T(8,128)S(1)}, f32[4,128,16]{1,2,0:T(8,128)S(1)}) fusion(pred[4,128]{1,0:T(4,128)(4,1)S(1)} %iota_compare_fusion.4, pred[16,128]{1,0:T(8,128)(4,1)S(1)} %iota_compare_fusion.5, bf16[16,128,512]{2,1,0:T(8,128)(2,1)} %get-tuple-element.188, bf16[16,4,128,512]{3,2,1,0:T(8,128)(2,1)} %get-tuple-element.187, ...), kind=kOutput, calls=%fused_computation.clone.1 | convolution fusion | flops 1077919744 | bytes 2690048 | tf_op jit(solution)/shard_map/while/body/eval_jaxpr/ape,bqe->abpq/dot_general | solution.py:25
  233.2 3.3 %select_reduce_fusion.4 = (f32[4,16,128]{2,1,0:T(8,128)S(1)}, f32[4,128,16]{1,2,0:T(8,128)S(1)}) fusion(pred[4,128]{1,0:T(4,128)(4,1)S(1)} %iota_compare_fusion.4, pred[16,128]{1,0:T(8,128)(4,1)S(1)} %iota_compare_fusion.5, bf16[16,128,512]{2,1,0:T(8,128)(2,1)} %get-tuple-element.188, bf16[16,4,128,512]{3,2,1,0:T(8,128)(2,1)} %get-tuple-element.187, ...), kind=kOutput, calls=%fused_computation.clone.1 | convolution fusion | flops 1077919744 | bytes 2690048 | tf_op jit(solution)/shard_map/while/body/eval_jaxpr/ape,bqe->abpq/dot_general | solution.py:25
  237.5 3.3 %select_reduce_fusion.4 = (f32[4,16,128]{2,1,0:T(8,128)S(1)}, f32[4,128,16]{1,2,0:T(8,128)S(1)}) fusion(pred[4,128]{1,0:T(4,128)(4,1)S(1)} %iota_compare_fusion.4, pred[16,128]{1,0:T(8,128)(4,1)S(1)} %iota_compare_fusion.5, bf16[16,128,512]{2,1,0:T(8,128)(2,1)} %get-tuple-element.188, bf16[16,4,128,512]{3,2,1,0:T(8,128)(2,1)} %get-tuple-element.187, ...), kind=kOutput, calls=%fused_computation.clone.1 | convolution fusion | flops 1077919744 | bytes 2690048 | tf_op jit(solution)/shard_map/while/body/eval_jaxpr/ape,bqe->abpq/dot_general | solution.py:25
  241.8 3.3 %select_reduce_fusion.4 = (f32[4,16,128]{2,1,0:T(8,128)S(1)}, f32[4,128,16]{1,2,0:T(8,128)S(1)}) fusion(pred[4,128]{1,0:T(4,128)(4,1)S(1)} %iota_compare_fusion.4, pred[16,128]{1,0:T(8,128)(4,1)S(1)} %iota_compare_fusion.5, bf16[16,128,512]{2,1,0:T(8,128)(2,1)} %get-tuple-element.188, bf16[16,4,128,512]{3,2,1,0:T(8,128)(2,1)} %get-tuple-element.187, ...), kind=kOutput, calls=%fused_computation.clone.1 | convolution fusion | flops 1077919744 | bytes 2690048 | tf_op jit(solution)/shard_map/while/body/eval_jaxpr/ape,bqe->abpq/dot_general | solution.py:25
  246.0 3.3 %select_reduce_fusion.4 = (f32[4,16,128]{2,1,0:T(8,128)S(1)}, f32[4,128,16]{1,2,0:T(8,128)S(1)}) fusion(pred[4,128]{1,0:T(4,128)(4,1)S(1)} %iota_compare_fusion.4, pred[16,128]{1,0:T(8,128)(4,1)S(1)} %iota_compare_fusion.5, bf16[16,128,512]{2,1,0:T(8,128)(2,1)} %get-tuple-element.188, bf16[16,4,128,512]{3,2,1,0:T(8,128)(2,1)} %get-tuple-element.187, ...), kind=kOutput, calls=%fused_computation.clone.1 | convolution fusion | flops 1077919744 | bytes 2690048 | tf_op jit(solution)/shard_map/while/body/eval_jaxpr/ape,bqe->abpq/dot_general | solution.py:25
  (116 shorter events, 17.9 us)
Async XLA Ops:
  7.2 1.1 copy-start
  7.2 106.4 %copy-start.2 = (u32[256]{0:T(256)S(1)}, u32[256]{0:T(256)}, u32[]{:S(2)}) copy-start(u32[256]{0:T(256)} %constant.82) | copy-start | bytes 3076
  7.2 107.7 %copy-start.1 = (s32[2]{0:T(128)S(1)}, s32[2]{0:T(128)}, u32[]{:S(2)}) copy-start(s32[2]{0:T(128)} %param.6) | copy-start | bytes 28
  7.2 103.3 %all-gather.2.cloned.1.call-start = ((), (), s32[]{:S(2)}) async-start(), calls=%async_computation | async-start | bytes 8650752 | tf_op jit(solution)/shard_map/all_gather | solution.py:41
  10.6 171.1 %all-reduce.3.cloned.1.call-start = ((), (), s32[]{:S(2)}) async-start(), calls=%async_computation.1 | async-start | bytes 4194304 | tf_op jit(solution)/shard_map/psum | solution.py:11
Sparse Core Ops, SparseCore 0:
  11.2 99.2 all-gather.1
  113.7 67.9 all-reduce.2
where the time goes:
time: 260 us; the launch traced here: 258 us
  waiting for transfers between devices  141 us (54%)
  matrix products  54.4 us (21%)
  blocking collectives  25.8 us (10%)
  other arithmetic  19.2 us (7%)
  between operations  14.8 us (6%)
  local copies, waits for them, and re-layouts  2.69 us (1%)
    all_gather x1, waiting for transfers between devices, on_device(): lax.all_gather(own, 'dev', axis=0, tiled=True)  99.8 us
    dot_general x16, matrix products, score_block(): jnp.einsum('ape,bqe->abpq', rows, cols, preferred_element_type=jnp.float32)  52.9 us
    psum x1, waiting for transfers between devices, spread(): return lax.psum(jnp.where(mine, value, jnp.zeros_like(value)), axis)  40.7 us
    unnamed x1, blocking collectives  13.3 us
    psum x1, blocking collectives, spread(): return lax.psum(jnp.where(mine, value, jnp.zeros_like(value)), axis)  12.5 us
    dynamic_update_slice x32, other arithmetic, on_device(): forward, chamfer = lax.map(one_block, (blocks, block_counts))  11.3 us
  transfers between devices with their start and end apart: 2, of which 2 were waited for; matrix products, arithmetic and copies ran while one was open for 0% of the time, Pallas kernels for 0%

commit v1 on v0

v1 whole, which is shorter than its diff:
```python
import functools

import jax
import jax.numpy as jnp
from jax import lax
from jax.experimental import pallas as pl
from jax.experimental.pallas import tpu as pltpu
from jax.sharding import PartitionSpec as P

MESH = pl.DeviceIdType.MESH

NX, NY, NZ = 4, 4, 8
SLOTS = 128
KEEP = 120
SHARD = 2 * KEEP
CUT = (0, 128, SHARD)

PLUS = ((0, 3, 0), (1, 3, 0), (0, 2, 0), (1, 3, 3), (1, 3, 1), (1, 2, 0), (1, 3, 2), (1, 2, 1))
MINUS = ((0, 1, 0), (1, 1, 0), (1, 1, 1), (1, 1, 3), (1, 1, 2), (1, 2, 3), (1, 2, 2))


def swapped(pieces):
    return tuple((1 - piece, oy, ox) for piece, ox, oy in pieces)


LINKS = {(1, 0): PLUS, (-1, 0): MINUS, (0, 1): swapped(PLUS), (0, -1): swapped(MINUS)}


def sends_of(piece, ox, oy):
    out = []
    for (dx, dy), pieces in LINKS.items():
        if (piece, (ox - dx) % NX, (oy - dy) % NY) in pieces:
            out.append((dx, dy))
    return out


def arrivals():
    rounds = []
    for turn in range(max(len(p) for p in LINKS.values())):
        rounds.append([(d, p[turn]) for d, p in LINKS.items() if turn < len(p)])
    return rounds


def kernel(features, counts, projection, out, chamfer, emb, mine, rows, cols, best, gsum, gsumt, gline, gback, *sems):
    (row_send, row_recv, col_send, col_recv, twin_send, twin_recv, shuf_send, shuf_recv, out_send, out_recv, line_send, line_recv, back_send, back_recv) = sems
    grp, dev = lax.axis_index("grp"), lax.axis_index("dev")
    y, c = grp // 2, grp % 2
    x, z = dev // NZ, dev % NZ
    sign = 1 - 2 * c

    def device(x, y, z, c):
        return (y * 2 + c, x * NZ + z)

    def near(dx=0, dy=0, dz=0):
        return device((x + sign * dx + NX) % NX, (y + sign * dy + NY) % NY, (z + sign * dz + NZ) % NZ, c)

    twin = device(x, y, z, 1 - c)
    shuffle_to = device(z % NX, y, x + NX * c, z // NX)
    shuffle_self = z == x + NX * c
    special = jnp.logical_and(shuffle_self, x == y)

    barrier = pltpu.get_barrier_semaphore()

    def greet(target):
        pl.semaphore_signal(barrier, inc=1, device_id=target, device_id_type=MESH)

    for k in range(NX):
        @pl.when(jnp.logical_not(jnp.logical_and(special, z % NX == k)))
        def _():
            greet(device(z % NX, x, k + NX * c, z // NX))

    @pl.when(jnp.logical_not(shuffle_self))
    def _():
        greet(shuffle_to)

    for step in ((1, 0, 0), (-1, 0, 0), (2, 0, 0), (0, 1, 0), (0, -1, 0), (0, 0, 1), (0, 0, -1)):
        greet(near(*step))
    greet(twin)

    raw = jnp.dot(features[...].reshape(2 * SLOTS, -1), projection[...], preferred_element_type=jnp.float32)
    scale = lax.rsqrt(jnp.sum(raw * raw, axis=1, keepdims=True) + 1e-06)
    embed = (raw * scale).astype(jnp.bfloat16).astype(jnp.float32)
    slot = lax.broadcasted_iota(jnp.int32, (SLOTS, 1), 0)
    for s in range(2):
        block = embed[s * SLOTS:(s + 1) * SLOTS]
        valid = slot < counts[s]
        count = jnp.where(slot == SLOTS - 1, counts[s].astype(jnp.float32), 0.0)
        rows[z, s] = jnp.where(valid, block, count).astype(jnp.bfloat16)
        emb[pl.ds(s * KEEP, KEEP), :] = jnp.where(valid, block, block[0:1])[:KEEP]
    mine[...] = emb[...].astype(jnp.bfloat16)

    pl.semaphore_wait(barrier, 13 - shuffle_self.astype(jnp.int32) - special.astype(jnp.int32))

    pending = []

    def remote(src, dst, send, recv, target):
        copy = pltpu.make_async_remote_copy(src_ref=src, dst_ref=dst, send_sem=send, recv_sem=recv, device_id=target, device_id_type=MESH)
        copy.start()
        pending.append(copy)

    def arrived(ref, sem):
        pltpu.make_async_copy(ref, ref, sem).wait()

    def shuffle_copy(piece):
        part = pl.ds(CUT[piece], CUT[piece + 1] - CUT[piece])
        return pltpu.make_async_remote_copy(
            src_ref=mine.at[part], dst_ref=cols.at[z // NX, y, z % NX, part],
            send_sem=shuf_send.at[piece], recv_sem=shuf_recv.at[piece], device_id=shuffle_to, device_id_type=MESH)

    @pl.when(jnp.logical_not(shuffle_self))
    def _():
        shuffle_copy(0).start()
        shuffle_copy(1).start()

    @pl.when(shuffle_self)
    def _():
        cols[c, y, x] = mine[...]

    ring_index = {}

    def ring_send(offset, half, way):
        key = ((offset - way), half)
        index = ring_index.setdefault(key, len(ring_index))
        ref = rows.at[(z + sign * offset + NZ) % NZ, half]
        remote(ref, ref, row_send.at[index], row_recv.at[index], near(0, 0, way))

    def ring_wait(offset, half):
        arrived(rows.at[(z + sign * offset + NZ) % NZ, half], row_recv.at[ring_index[(offset, half)]])

    for half in range(2):
        for way in (1, -1):
            ring_send(0, half, way)

    col_index = {}

    def col_ref(piece, ox, oy):
        part = pl.ds(CUT[piece], CUT[piece + 1] - CUT[piece])
        return cols.at[c, (y + sign * oy + NY) % NY, (x + sign * ox + NX) % NX, part]

    def col_key(piece, ox, oy):
        return col_index.setdefault((piece, ox % NX, oy % NY), len(col_index))

    def pass_on(piece, ox, oy):
        for dx, dy in sends_of(piece, ox, oy):
            index = col_key(piece, ox - dx, oy - dy)
            ref = col_ref(piece, ox, oy)
            remote(ref, ref, col_send.at[index], col_recv.at[index], near(dx, dy, 0))

    def to_twin(ox, oy):
        index = ox * NY + oy
        ref = cols.at[c, (y + sign * oy + NY) % NY, (x + sign * ox + NX) % NX]
        remote(ref, ref, twin_send.at[index], twin_recv.at[index], twin)

    def from_twin(ox, oy):
        index = (-ox % NX) * NY + (-oy % NY)
        arrived(cols.at[1 - c, (y + sign * oy + NY) % NY, (x + sign * ox + NX) % NX], twin_recv.at[index])

    for piece in range(2):
        @pl.when(jnp.logical_not(shuffle_self))
        def _():
            shuffle_copy(piece).wait_recv()

        pass_on(piece, 0, 0)
    to_twin(0, 0)

    have = {}
    ring_order = [[(o * way, h) for way in (-1, 1)] for o in (1, 2, 3) for h in (0, 1)] + [[(-4, 0), (4, 1)]]
    for turn, pieces in enumerate(arrivals()):
        for _, (piece, ox, oy) in pieces:
            arrived(col_ref(piece, ox, oy), col_recv.at[col_key(piece, ox, oy)])
            pass_on(piece, ox, oy)
            have.setdefault((ox, oy), []).append(piece)
            if len(have[(ox, oy)]) == 2:
                to_twin(ox, oy)
        if turn < len(ring_order):
            for offset, half in ring_order[turn]:
                ring_wait(offset, half)
                way = 1 if offset < 0 else -1
                if abs(offset) < 3 or (abs(offset) == 3 and half == (0 if way == 1 else 1)):
                    ring_send(offset, half, way)
    for ox in range(NX):
        for oy in range(NY):
            from_twin(ox, oy)

    lane = lax.broadcasted_iota(jnp.int32, (1, SLOTS), 1)

    def unit(i, carry):
        column, half = i // 2, i % 2
        block = cols[half, column].reshape(NX * SHARD, -1)
        for ring in range(NZ):
            score = lax.dot_general(block, rows[ring].reshape(2 * SLOTS, -1), (((1,), (1,)), ((), ())), preferred_element_type=jnp.float32)
            top = jnp.max(score.reshape(2 * NX, KEEP, 2 * SLOTS), axis=1)
            for s in range(2):
                best[column, 2 * ring + s, pl.ds(pl.multiple_of(half * 8, 8), 8), :] = jnp.where(lane < KEEP, top[:, s * SLOTS:(s + 1) * SLOTS], 0.0)
        return carry

    lax.fori_loop(0, 2 * NY, unit, 0)

    for column in range(NY):
        for ring in range(NZ):
            for s in range(2):
                a = 2 * ring + s
                count = rows[ring, s, pl.ds(SLOTS - 16, 16), 0:1].astype(jnp.float32)[15:16]
                gsumt[column, :, a:a + 1] = jnp.sum(best[column, a], axis=1, keepdims=True) / count
        gsum[column, :, 0:16] = gsumt[column, :, 0:16].T

    def back_copy(k):
        return pltpu.make_async_remote_copy(
            src_ref=gsumt.at[k], dst_ref=gback.at[z % NX], send_sem=back_send.at[k], recv_sem=back_recv.at[z % NX],
            device_id=device(y, k, x + NX * c, z // NX), device_id_type=MESH)

    for k in range(NY):
        here = jnp.logical_and(special, y == k)

        @pl.when(jnp.logical_not(here))
        def _():
            back_copy(k).start()

        @pl.when(here)
        def _():
            gback[z % NX] = gsumt[k]

    for d in (1, 3, 2):
        column = (x + d) % NX
        to = device(column, y, z, c)
        remote(gsum.at[column], gline.at[x], line_send.at[d], line_recv.at[d], to)
        remote(best.at[column], out.at[pl.ds(16 * x, 16)], out_send.at[d], out_recv.at[d], to)
    gline[x] = gsum[x]
    out[pl.ds(16 * x, 16)] = best[x]

    for d in (1, 3, 2):
        source = (x - d + NX) % NX
        arrived(gline.at[source], line_recv.at[d])
    for k in range(NX):
        @pl.when(jnp.logical_not(jnp.logical_and(special, z % NX == k)))
        def _():
            arrived(gback.at[k], back_recv.at[k])
    for k in range(NX):
        chamfer[pl.ds(16 * k, 16), :] = 0.5 * (gline[k][:, 0:16] + gback[k][:, 0:16])
    for d in (1, 3, 2):
        source = (x - d + NX) % NX
        arrived(out.at[pl.ds(16 * source, 16)], out_recv.at[d])

    for copy in pending:
        copy.wait_send()

    @pl.when(jnp.logical_not(shuffle_self))
    def _():
        shuffle_copy(0).wait_send()
        shuffle_copy(1).wait_send()

    for k in range(NY):
        @pl.when(jnp.logical_not(jnp.logical_and(special, y == k)))
        def _():
            back_copy(k).wait_send()


def on_device(features, tile_counts, projection):
    dma = pltpu.SemaphoreType.DMA
    width = projection.shape[1]
    vmem = pl.BlockSpec(memory_space=pltpu.VMEM)
    return pl.pallas_call(
        kernel,
        name="chamfer",
        out_shape=(jax.ShapeDtypeStruct((64, 16, SLOTS), jnp.float32), jax.ShapeDtypeStruct((64, 16), jnp.float32)),
        in_specs=[vmem, pl.BlockSpec(memory_space=pltpu.SMEM), vmem],
        out_specs=(vmem, vmem),
        scratch_shapes=[
            pltpu.VMEM((SHARD, width), jnp.float32),
            pltpu.VMEM((SHARD, width), jnp.bfloat16),
            pltpu.VMEM((NZ, 2, SLOTS, width), jnp.bfloat16),
            pltpu.VMEM((2, NY, NX, SHARD, width), jnp.bfloat16),
            pltpu.VMEM((NY, 16, 16, SLOTS), jnp.float32),
            pltpu.VMEM((NY, 16, SLOTS), jnp.float32),
            pltpu.VMEM((NY, 16, SLOTS), jnp.float32),
            pltpu.VMEM((NX, 16, SLOTS), jnp.float32),
            pltpu.VMEM((NX, 16, SLOTS), jnp.float32),
            dma((14,)), dma((14,)), dma((30,)), dma((30,)), dma((16,)), dma((16,)), dma((2,)), dma((2,)),
            dma((4,)), dma((4,)), dma((4,)), dma((4,)), dma((4,)), dma((4,)),
        ],
        compiler_params=pltpu.CompilerParams(collective_id=0, has_side_effects=True, vmem_limit_bytes=48 * 2**20),
    )(features, tile_counts, projection)


def solution(mesh):
    return jax.shard_map(
        on_device,
        mesh=mesh,
        in_specs=(P(("grp", "dev"), None, None), P(("grp", "dev")), P()),
        out_specs=(P("grp", "dev", None), P("grp", "dev")),
        check_vma=False,
    )
```

time: 260 us -> 88.9 us (0.34)
  the two profiles are of different devices: /device:TPU:5 before, /device:TPU:65 now
where the time goes in v1:
time: 88.9 us; the launch traced here: 88.8 us
  Pallas kernels  83.9 us (94%)
  local copies, waits for them, and re-layouts  4.24 us (5%)
    pallas_call x1, Pallas kernels, on_device(): pl.pallas_call(kernel, name='chamfer', out_shape=(jax.ShapeDtypeStruct((6...  83.9 us
    unnamed x7, local copies, waits for them, and re-layouts  3.57 us

profile of v1, /device:TPU:65, one launch (start us, length us, event | category | flops | bytes accessed | tf_op | source)
XLA Modules:
  0.0 88.8 jit_solution(8752951318740859344)
XLA Ops:
  0.6 0.0 copy-start
  0.6 1.1 %copy-done = bf16[768,512]{1,0:T(8,128)(2,1)S(1)} copy-done((bf16[768,512]{1,0:T(8,128)(2,1)S(1)}, bf16[768,512]{1,0:T(8,128)(2,1)}, u32[]{:S(2)}) %copy-start) | copy-done | bytes 786456
  1.8 0.0 copy-start.1
  1.8 1.0 %copy-done.1 = bf16[2,128,768]{2,1,0:T(8,128)(2,1)S(1)} copy-done((bf16[2,128,768]{2,1,0:T(8,128)(2,1)S(1)}, bf16[2,128,768]{2,1,0:T(8,128)(2,1)}, u32[]{:S(2)}) %copy-start.1) | copy-done | bytes 393240
  2.8 0.0 copy-start.2
  2.8 0.7 copy-done.2
  3.4 83.9 %chamfer.1 = (f32[64,16,128]{2,1,0:T(8,128)S(1)}, f32[64,16]{1,0:T(8,128)S(1)}) custom-call(bf16[2,128,768]{2,1,0:T(8,128)(2,1)S(1)} %copy-done.1, s32[2]{0:T(128)S(1)} %copy-done.2, bf16[768,512]{1,0:T(8,128)(2,1)S(1)} %copy-done), custom_call_target="tpu_custom_call" | custom-call | tf_op jit(solution)/shard_map/chamfer/pallas_call | solution.py:262
  87.3 0.7 copy.5
  88.0 0.8 copy.7
Async XLA Ops:
  0.6 1.1 %copy-start = (bf16[768,512]{1,0:T(8,128)(2,1)S(1)}, bf16[768,512]{1,0:T(8,128)(2,1)}, u32[]{:S(2)}) copy-start(bf16[768,512]{1,0:T(8,128)(2,1)} %projection.1) | copy-start | bytes 2359300
  1.8 1.0 %copy-start.1 = (bf16[2,128,768]{2,1,0:T(8,128)(2,1)S(1)}, bf16[2,128,768]{2,1,0:T(8,128)(2,1)}, u32[]{:S(2)}) copy-start(bf16[2,128,768]{2,1,0:T(8,128)(2,1)} %features.1) | copy-start | bytes 1179652
  2.8 0.7 copy-start.2

commit v2 on v0

v2 whole, which is shorter than its diff:
```python
import jax
import jax.numpy as jnp
from jax import lax
from jax.experimental import pallas as pl
from jax.experimental.pallas import tpu as pltpu
from jax.sharding import PartitionSpec as P

MESH = pl.DeviceIdType.MESH

NX, NY, NZ = 4, 4, 8
SLOTS = 128
KEEP = 120
SHARD = 2 * KEEP
PIECES = ((0, 0, 128), (1, 128, 240))

T_RING, D_RING = 1.5, 2.75
T_COL, D_COL = 1.5, 2.9
T_TWIN = 1.5
T_TILE, T_BLOCK = 0.075, 0.1


def per_piece(entries):
    return tuple((p, ox, oy) for way, ox, oy in entries for p, piece in enumerate(PIECES) if piece[0] == way)


PLUS = ((0, 3, 0), (1, 3, 0), (0, 2, 0), (1, 3, 3), (1, 3, 1), (1, 2, 0), (1, 3, 2), (1, 2, 1))
MINUS = ((0, 1, 0), (1, 1, 0), (1, 1, 1), (1, 1, 3), (1, 1, 2), (1, 2, 3), (1, 2, 2))


def swapped(entries):
    return tuple((1 - way, oy, ox) for way, ox, oy in entries)


LINKS = {(1, 0): per_piece(PLUS), (-1, 0): per_piece(MINUS), (0, 1): per_piece(swapped(PLUS)), (0, -1): per_piece(swapped(MINUS))}
MOST = 8
WAY_PIECES = max(sum(1 for p in PIECES if p[0] == way) for way in range(2))


def sends_of(p, ox, oy):
    return [(dx, dy) for (dx, dy), pieces in LINKS.items() if (p, (ox - dx) % NX, (oy - dy) % NY) in pieces]


def plan():
    times = {}
    for pieces in LINKS.values():
        for i, key in enumerate(pieces):
            times[key] = T_COL + D_COL * (i + 1) / WAY_PIECES
    events = [(t, "col", key) for key, t in times.items()]
    for p in range(len(PIECES)):
        times[(p, 0, 0)] = 0.0
    ready = {}
    for ox in range(NX):
        for oy in range(NY):
            t = max(times[(p, ox, oy)] for p in range(len(PIECES)))
            twin = (1, -ox % NX, -oy % NY)
            ready[(0, ox, oy)] = t
            ready[twin] = t + T_TWIN
            events.append((t + 0.001, "to_twin", (ox, oy)))
            events.append((t + T_TWIN, "twin", twin[1:]))
    tile_ready = {0: 0.0}
    for slot, halves in enumerate([[(o * way, h) for way in (-1, 1)] for o in (1, 2, 3) for h in (0, 1)] + [[(-4, 0), (4, 1)]]):
        for offset, half in halves:
            t = T_RING + D_RING * (slot + 1)
            events.append((t, "ring", (offset, half)))
            tile = 4 if abs(offset) == 4 else offset
            tile_ready[tile] = max(t, tile_ready.get(tile, 0.0))
    events.sort(key=lambda e: e[0])
    todo = {shard: set(tile_ready) for shard in ready}
    order = [(core, oy) for oy in (0, 3, 1, 2) for core in (0, 1)]
    program, now = [], 0.0
    while events or todo:
        while events and events[0][0] <= now:
            program.append(("event",) + events.pop(0)[1:])
            now += 0.05
        best = None
        for shard, tiles in todo.items():
            if ready[shard] > now:
                continue
            usable = sorted(t for t in tiles if tile_ready[t] <= now)
            if not usable or (len(usable) < 2 and len(usable) < len(tiles)):
                continue
            if events:
                usable = usable[:MOST]
            rank = (len(usable) == len(tiles), -order.index((shard[0], shard[2])), len(usable))
            if best is None or rank > best[0]:
                best = (rank, shard, usable)
        if best is None:
            now = max(now, events[0][0])
            continue
        _, shard, usable = best
        program.append(("block", shard, tuple(usable)))
        now += T_BLOCK + T_TILE * len(usable)
        todo[shard] -= set(usable)
        if not todo[shard]:
            del todo[shard]
            program.append(("done", shard))
            now += 0.1
    return program, now


def kernel(features_hbm, counts, projection_hbm, taken, back, features, projection, emb, rows, cols, best, count, means, *sems):
    load, row_send, row_recv, col_send, col_recv, twin_send, twin_recv, out_send, out_recv, back_send, back_recv = sems
    grp, dev = lax.axis_index("grp"), lax.axis_index("dev")
    y, c = grp // 2, grp % 2
    x, z = dev // NZ, dev % NZ
    sign = 1 - 2 * c

    def device(x, y, z, c):
        return (y * 2 + c, x * NZ + z)

    def near(dx=0, dy=0, dz=0):
        return device((x + sign * dx + NX) % NX, (y + sign * dy + NY) % NY, (z + sign * dz + NZ) % NZ, c)

    twin = device(x, y, z, 1 - c)
    special = jnp.logical_and(z == x + NX * c, x == y)

    barrier = pltpu.get_barrier_semaphore()

    def greet(target):
        pl.semaphore_signal(barrier, inc=1, device_id=target, device_id_type=MESH)

    def back_source(k):
        return jnp.logical_and(special, z == k)

    for k in range(NZ):
        @pl.when(jnp.logical_not(back_source(k)))
        def _():
            greet(device(z % NX, x, k, z // NX))

    for dx in range(NX):
        for dz in range(NZ):
            if (dx, dz) != (0, 0):
                greet(device((x + dx) % NX, y, (z + dz) % NZ, c))
    greet(near(0, 1, 0))
    greet(near(0, -1, 0))
    greet(twin)

    load_features = pltpu.make_async_copy(features_hbm, features, load.at[0])
    load_projection = pltpu.make_async_copy(projection_hbm, projection, load.at[1])
    load_features.start()
    load_projection.start()
    load_features.wait()
    load_projection.wait()

    raw = jnp.dot(features[...].reshape(2 * SLOTS, -1), projection[...], preferred_element_type=jnp.float32)
    scale = lax.rsqrt(jnp.sum(raw * raw, axis=1, keepdims=True) + 1e-06)
    embed = (raw * scale).astype(jnp.bfloat16).astype(jnp.float32)
    slot = lax.broadcasted_iota(jnp.int32, (SLOTS, 1), 0)
    for s in range(2):
        block = embed[s * SLOTS:(s + 1) * SLOTS]
        valid = slot < counts[s]
        number = jnp.where(slot == SLOTS - 1, counts[s].astype(jnp.float32), 0.0)
        rows[z, s] = jnp.where(valid, block, number).astype(jnp.bfloat16)
        emb[pl.ds(s * KEEP, KEEP), :] = jnp.where(valid, block, block[0:1])[:KEEP]
    cols[y, x, c] = emb[...].astype(jnp.bfloat16)
    means[...] = jnp.zeros_like(means)

    pl.semaphore_wait(barrier, (NX * NZ - 1) + 3 + NZ - special.astype(jnp.int32))

    pending = []

    def remote(src, dst, send, recv, target):
        copy = pltpu.make_async_remote_copy(src_ref=src, dst_ref=dst, send_sem=send, recv_sem=recv, device_id=target, device_id_type=MESH)
        copy.start()
        pending.append(copy)

    def arrived(ref, sem):
        pltpu.make_async_copy(ref, ref, sem).wait()

    ring_index = {}

    def ring_ref(offset, half):
        return rows.at[(z + sign * offset + NZ) % NZ, half]

    def ring_send(offset, half, way):
        index = ring_index.setdefault((offset - way, half), len(ring_index))
        ref = ring_ref(offset, half)
        remote(ref, ref, row_send.at[index], row_recv.at[index], near(0, 0, way))

    def ring_event(offset, half):
        arrived(ring_ref(offset, half), row_recv.at[ring_index[(offset, half)]])
        way = 1 if offset < 0 else -1
        if abs(offset) < 3 or (abs(offset) == 3 and half == (0 if way == 1 else 1)):
            ring_send(offset, half, way)

    col_index = {}

    def place(core, ox, oy):
        return (y + sign * oy + NY) % NY, (x + sign * ox + NX) % NX, (c if core == 0 else 1 - c)

    def col_ref(p, ox, oy):
        return cols.at[(*place(0, ox, oy), pl.ds(PIECES[p][1], PIECES[p][2] - PIECES[p][1]))]

    def col_key(p, ox, oy):
        return col_index.setdefault((p, ox % NX, oy % NY), len(col_index))

    def pass_on(p, ox, oy):
        for dx, dy in sends_of(p, ox, oy):
            index = col_key(p, ox - dx, oy - dy)
            ref = col_ref(p, ox, oy)
            remote(ref, ref, col_send.at[index], col_recv.at[index], near(dx, dy, 0))

    def col_event(p, ox, oy):
        arrived(col_ref(p, ox, oy), col_recv.at[col_key(p, ox, oy)])
        pass_on(p, ox, oy)

    def to_twin_event(ox, oy):
        index = ox * NY + oy
        ref = cols.at[place(0, ox, oy)]
        remote(ref, ref, twin_send.at[index], twin_recv.at[index], twin)

    def twin_event(ox, oy):
        arrived(cols.at[place(1, ox, oy)], twin_recv.at[(-ox % NX) * NY + (-oy % NY)])

    def block_step(core, ox, oy, tiles):
        where = place(core, ox, oy)
        block = cols[where]
        for tile in tiles:
            ring = (z + sign * tile + NZ) % NZ
            score = lax.dot_general(block, rows[ring].reshape(2 * SLOTS, -1), (((1,), (1,)), ((), ())), preferred_element_type=jnp.float32)
            for b in range(2):
                top = jnp.max(score[b * KEEP:(b + 1) * KEEP], axis=0, keepdims=True)
                for s in range(2):
                    best[(*where, b, pl.ds(2 * ring + s, 1))] = top[:, s * SLOTS:(s + 1) * SLOTS]

    lane = lax.broadcasted_iota(jnp.int32, (1, SLOTS), 1)

    def out_copy(core, ox, oy):
        column, line, half = place(core, ox, oy)
        index = (core * NX + ox) * NY + oy
        return pltpu.make_async_remote_copy(
            src_ref=best.at[column, line, half], dst_ref=taken.at[x, z], send_sem=out_send.at[index], recv_sem=out_recv.at[x * NZ + z],
            device_id=device(column, y, line + NX * half, c), device_id_type=MESH)

    def out_here(core, ox, oy):
        column, line, half = place(core, ox, oy)
        return jnp.logical_and(column == x, line + NX * half == z)

    def back_copy(core, oy):
        column, _, half = place(core, 0, oy)
        return pltpu.make_async_remote_copy(
            src_ref=means.at[column, half], dst_ref=back.at[z], send_sem=back_send.at[core * NY + oy], recv_sem=back_recv.at[z],
            device_id=device(y, column, x + NX * c, half), device_id_type=MESH)

    def back_here(core, oy):
        column, _, half = place(core, 0, oy)
        return jnp.logical_and(special, jnp.logical_and(column == y, half == c))

    finished = {}

    def done_step(core, ox, oy):
        if not finished:
            for a in range(2 * NZ):
                count[a:a + 1] = rows[a // 2, a % 2, pl.ds(SLOTS - 16, 16), 0:SLOTS].astype(jnp.float32)[15:16]
        where = place(core, ox, oy)
        column, line, half = where
        mean = means[column, half]
        for b in range(2):
            top = jnp.where(lane < KEEP, best[(*where, b)], 0.0)
            value = jnp.sum(top, axis=1, keepdims=True) / count[...]
            best[(*where, b)] = jnp.where(lane == SLOTS - 1, value, top)
            mean = jnp.where(lane == 2 * line + b, value, mean)
        means[column, half] = mean

        @pl.when(jnp.logical_not(out_here(core, ox, oy)))
        def _():
            out_copy(core, ox, oy).start()

        @pl.when(out_here(core, ox, oy))
        def _():
            taken[x, z] = best[where]

        group = finished.setdefault((core, oy), [])
        group.append(ox)
        if len(group) == NX:
            @pl.when(jnp.logical_not(back_here(core, oy)))
            def _():
                back_copy(core, oy).start()

            @pl.when(back_here(core, oy))
            def _():
                back[z] = means[column, half]

    for p in range(len(PIECES)):
        pass_on(p, 0, 0)
        if p == 0:
            for half in range(2):
                for way in (1, -1):
                    ring_send(0, half, way)
    handlers = {"col": col_event, "ring": ring_event, "to_twin": to_twin_event, "twin": twin_event}
    for entry in plan()[0]:
        if entry[0] == "event":
            handlers[entry[1]](*entry[2])
        elif entry[0] == "block":
            block_step(*entry[1], entry[2])
        else:
            done_step(*entry[1])

    for k in range(NZ):
        @pl.when(jnp.logical_not(back_source(k)))
        def _():
            arrived(back.at[k], back_recv.at[k])
    for i in range(NX):
        for k in range(NZ):
            @pl.when(jnp.logical_not(jnp.logical_and(x == i, z == k)))
            def _():
                arrived(taken.at[i, k], out_recv.at[i * NZ + k])

    for copy in pending:
        copy.wait_send()
    for core in range(2):
        for oy in range(NY):
            @pl.when(jnp.logical_not(back_here(core, oy)))
            def _():
                back_copy(core, oy).wait_send()

            for ox in range(NX):
                @pl.when(jnp.logical_not(out_here(core, ox, oy)))
                def _():
                    out_copy(core, ox, oy).wait_send()


def place_kernel(taken, back, out, chamfer, turned):
    lane = lax.broadcasted_iota(jnp.int32, (1, SLOTS), 1)
    for k in range(NZ):
        turned[...] = back[k].T
        for i in range(NX):
            chamfer[pl.ds(16 * i + 2 * k, 2), :] = turned[pl.ds(2 * i, 2), :]
    for i in range(NX):
        line = jnp.zeros((16, SLOTS), jnp.float32)
        for k in range(NZ):
            for b in range(2):
                value = taken[i, k, b]
                line = jnp.where(lane == 2 * k + b, value[:, SLOTS - 1:SLOTS], line)
                out[pl.ds(16 * i, 16), 2 * k + b, :] = jnp.where(lane < KEEP, value, 0.0)
        part = pl.ds(16 * i, 16)
        chamfer[part, :] = 0.5 * (chamfer[part, :] + line[:, 0:16])


def on_device(features, tile_counts, projection):
    dma = pltpu.SemaphoreType.DMA
    width = projection.shape[1]
    vmem = pl.BlockSpec(memory_space=pltpu.VMEM)
    anywhere = pl.BlockSpec(memory_space=pl.ANY)
    pieces = len(PIECES)
    f32 = jnp.float32
    taken, back = pl.pallas_call(
        kernel,
        name="compare",
        out_shape=(jax.ShapeDtypeStruct((NX, NZ, 2, 16, SLOTS), f32), jax.ShapeDtypeStruct((NZ, 16, SLOTS), f32)),
        in_specs=[anywhere, pl.BlockSpec(memory_space=pltpu.SMEM), anywhere],
        out_specs=(vmem, vmem),
        scratch_shapes=[
            pltpu.VMEM(features.shape, jnp.bfloat16),
            pltpu.VMEM(projection.shape, jnp.bfloat16),
            pltpu.VMEM((SHARD, width), f32),
            pltpu.VMEM((NZ, 2, SLOTS, width), jnp.bfloat16),
            pltpu.VMEM((NY, NX, 2, SHARD, width), jnp.bfloat16),
            pltpu.VMEM((NY, NX, 2, 2, 16, SLOTS), f32),
            pltpu.VMEM((16, SLOTS), f32),
            pltpu.VMEM((NY, 2, 16, SLOTS), f32),
            dma((2,)), dma((14,)), dma((14,)), dma((15 * pieces,)), dma((15 * pieces,)), dma((16,)), dma((16,)),
            dma((32,)), dma((32,)), dma((8,)), dma((8,)),
        ],
        compiler_params=pltpu.CompilerParams(collective_id=0, has_side_effects=True, vmem_limit_bytes=56 * 2**20),
    )(features, tile_counts, projection)
    return pl.pallas_call(
        place_kernel,
        name="place",
        out_shape=(jax.ShapeDtypeStruct((64, 16, SLOTS), f32), jax.ShapeDtypeStruct((64, 16), f32)),
        in_specs=[vmem, vmem],
        out_specs=(vmem, vmem),
        scratch_shapes=[pltpu.VMEM((SLOTS, 16), f32)],
    )(taken, back)


def solution(mesh):
    return jax.shard_map(
        on_device,
        mesh=mesh,
        in_specs=(P(("grp", "dev"), None, None), P(("grp", "dev")), P()),
        out_specs=(P("grp", "dev", None), P("grp", "dev")),
        check_vma=False,
    )
```

time: 260 us -> 71.7 us (0.28)
  waiting for transfers between devices: 141 us -> 0 us
  Pallas kernels: 0 us -> 69.4 us
  matrix products: 54.4 us -> 0 us
  blocking collectives: 25.8 us -> 0 us
  other arithmetic: 19.2 us -> 0 us
  between operations: 14.8 us -> 0.64 us
    all_gather x1 -> x0, waiting for transfers between devices: 99.8 us -> none  [on_device(): lax.all_gather(own, 'dev', axis=0, tiled=True)]
    pallas_call x0 -> x2, Pallas kernels: none -> 69.4 us  [the longest x1 67.1 us: on_device(): pl.pallas_call(kernel, name='compare', out_shape=(jax.ShapeDtypeStruct((N...]
    dot_general x17 -> x0, matrix products: 54.4 us -> none  [the longest x16 52.9 us: score_block(): jnp.einsum('ape,bqe->abpq', rows, cols, preferred_element_type=jnp.float32)]
    psum x1 -> x0, waiting for transfers between devices: 40.7 us -> none  [spread(): return lax.psum(jnp.where(mine, value, jnp.zeros_like(value)), axis)]
    unnamed x1 -> x0, blocking collectives: 13.3 us -> none
    psum x1 -> x0, blocking collectives: 12.5 us -> none  [spread(): return lax.psum(jnp.where(mine, value, jnp.zeros_like(value)), axis)]
    dynamic_update_slice x32 -> x0, other arithmetic: 11.3 us -> none  [on_device(): forward, chamfer = lax.map(one_block, (blocks, block_counts))]
    select_n x2 -> x0, other arithmetic: 3.1 us -> none  [spread(): return lax.psum(jnp.where(mine, value, jnp.zeros_like(value)), axis)]
  transfers between devices with their start and end apart: 2 -> 0, of which waited for: 2 -> 0; matrix products, arithmetic and copies ran while one was open for 0% -> 0% of each run, Pallas kernels for 0% -> 0%
where the time goes in v2:
time: 71.7 us; the launch traced here: 71.5 us
  Pallas kernels  69.4 us (97%)
  local copies, waits for them, and re-layouts  1.43 us (2%)
    pallas_call x1, Pallas kernels, on_device(): pl.pallas_call(kernel, name='compare', out_shape=(jax.ShapeDtypeStruct((N...  67.1 us
    pallas_call x1, Pallas kernels, on_device(): pl.pallas_call(place_kernel, name='place', out_shape=(jax.ShapeDtypeStruc...  2.27 us

profile of v2, /device:TPU:5, one launch (start us, length us, event | category | flops | bytes accessed | tf_op | source)
XLA Modules:
  0.0 71.5 jit_solution(9628653557847919983)
XLA Ops:
  0.6 67.1 %compare.1 = (f32[4,8,2,16,128]{4,3,2,1,0:T(8,128)}, f32[8,16,128]{2,1,0:T(8,128)}) custom-call(bf16[2,128,768]{2,1,0:T(8,128)(2,1)} %features_hbm.1, s32[2]{0:T(128)} %counts.1, bf16[768,512]{1,0:T(8,128)(2,1)} %projection_hbm.1), custom_call_target="tpu_custom_call" | custom-call | tf_op jit(solution)/shard_map/compare/pallas_call | solution.py:347
  67.8 2.3 %place.1 = (f32[64,16,128]{2,1,0:T(8,128)}, f32[64,16]{1,0:T(8,128)}) custom-call(f32[4,8,2,16,128]{4,3,2,1,0:T(8,128)} %get-tuple-element.4.taken, f32[8,16,128]{2,1,0:T(8,128)} %get-tuple-element.5.back), custom_call_target="tpu_custom_call" | custom-call | tf_op jit(solution)/shard_map/place/pallas_call | solution.py:367
  70.1 1.4 %copy.5 = f32[64,16]{0,1:T(8,128)} copy(f32[64,16]{1,0:T(8,128)} %get-tuple-element.7) | data formatting | bytes 8192 | tf_op jit(solution)/shard_map/place/pallas_call | solution.py:367

commit v3 on v2

v3 whole, which is shorter than its diff:
```python
import jax
import jax.numpy as jnp
from jax import lax
from jax.experimental import pallas as pl
from jax.experimental.pallas import tpu as pltpu
from jax.sharding import PartitionSpec as P

MESH = pl.DeviceIdType.MESH

NX, NY, NZ = 4, 4, 8
SLOTS = 128
KEEP = 120
SHARD = 2 * KEEP
PIECES = ((0, 0, 64), (0, 64, 128), (1, 128, 192), (1, 192, 240))
WAYS = ((0, 128), (128, 240))
QUARTER = 128
WINDOW = 2

T_ROW = 0.0213
T_HOP = 2.5
T_TWIN = 2.2
T_TILE, T_BLOCK, T_EVENT = 0.07, 0.1, 0.02
MOST = 4


def per_piece(entries):
    return tuple((p, ox, oy) for way, ox, oy in entries for p, piece in enumerate(PIECES) if piece[0] == way)


PLUS = ((0, 3, 0), (1, 3, 0), (0, 2, 0), (1, 3, 3), (1, 3, 1), (1, 2, 0), (1, 3, 2), (1, 2, 1))
MINUS = ((0, 1, 0), (1, 1, 0), (1, 1, 1), (1, 1, 3), (1, 1, 2), (1, 2, 3), (1, 2, 2))


def swapped(entries):
    return tuple((1 - way, oy, ox) for way, ox, oy in entries)


def ring_order(way):
    quarters = 2 * SLOTS // QUARTER
    whole = [(-way * o, q) for o in (1, 2, 3) for q in range(quarters)]
    return tuple(whole + [(4, q) for q in range(quarters) if (q < quarters // 2) == (way == 1)])


LINKS = {
    (1, 0, 0): tuple(("col", *k) for k in per_piece(PLUS)),
    (-1, 0, 0): tuple(("col", *k) for k in per_piece(MINUS)),
    (0, 1, 0): tuple(("col", *k) for k in per_piece(swapped(PLUS))),
    (0, -1, 0): tuple(("col", *k) for k in per_piece(swapped(MINUS))),
    (0, 0, 1): tuple(("row", *k) for k in ring_order(1)),
    (0, 0, -1): tuple(("row", *k) for k in ring_order(-1)),
}


def at_sender(link, key):
    dx, dy, dz = link
    if key[0] == "row":
        offset = key[1] + dz
        return ("row", offset - NZ if offset > 4 else offset, key[2])
    return ("col", key[1], (key[2] + dx) % NX, (key[3] + dy) % NY)


def length(key):
    return QUARTER if key[0] == "row" else PIECES[key[1]][2] - PIECES[key[1]][1]


def transfers():
    time = {("row", 0, q): 0.0 for q in range(2 * SLOTS // QUARTER)}
    time.update({("col", p, 0, 0): 0.0 for p in range(len(PIECES))})
    sent = {link: [] for link in LINKS}
    actions = []
    while True:
        nearest = None
        for link, keys in LINKS.items():
            i = len(sent[link])
            if i == len(keys) or at_sender(link, keys[i]) not in time:
                continue
            start = max(time[at_sender(link, keys[i])], sent[link][i - WINDOW] if i >= WINDOW else 0.0)
            if nearest is None or start < nearest[0]:
                nearest = (start, link, i)
        if nearest is None:
            return actions, time
        start, link, i = nearest
        key = LINKS[link][i]
        end = max(start, sent[link][-1] if sent[link] else 0.0) + length(key) * T_ROW
        sent[link].append(end)
        time[key] = end + T_HOP
        actions.append((start, 1, "send", (link, i)))
        actions.append((time[key], 0, "arrive", (link, i)))


def plan():
    events, time = transfers()
    ready = {}
    for ox in range(NX):
        for oy in range(NY):
            for way in range(2):
                t = max(time[("col", p, ox, oy)] for p, piece in enumerate(PIECES) if piece[0] == way)
                twin = (-ox % NX, -oy % NY)
                events.append((t, 2, "to_twin", (way, ox, oy)))
                events.append((t + T_TWIN, 0, "twin", (way, *twin)))
                ready[(0, ox, oy)] = max(ready.get((0, ox, oy), 0.0), t)
                ready[(1, *twin)] = max(ready.get((1, *twin), 0.0), t + T_TWIN)
    tile_ready = {tile: max(time[("row", tile, q)] for q in range(2 * SLOTS // QUARTER)) for tile in range(-3, 5)}
    events.sort(key=lambda e: e[:2])
    todo = {shard: set(tile_ready) for shard in ready}
    order = [(core, oy) for oy in (0, 3, 1, 2) for core in (0, 1)]
    program, now, late = [], 0.0, []
    while events or todo:
        while events and events[0][0] <= now:
            program.append((events[0][2], *events.pop(0)[3]))
            now += T_EVENT
        best = None
        for shard, tiles in todo.items():
            if ready[shard] > now:
                continue
            usable = sorted(t for t in tiles if tile_ready[t] <= now)
            if not usable or (len(usable) < 2 and len(usable) < len(tiles)):
                continue
            if events:
                usable = usable[:MOST]
            rank = (len(usable) == len(tiles), -order.index((shard[0], shard[2])), len(usable))
            if best is None or rank > best[0]:
                best = (rank, shard, usable)
        if best is None:
            now = max(now, events[0][0])
            continue
        _, shard, usable = best
        program.append(("block", shard, tuple(usable)))
        now += T_BLOCK + T_TILE * len(usable)
        todo[shard] -= set(usable)
        if not todo[shard]:
            del todo[shard]
        if late:
            program.append(("ship", late.pop()))
        group = shard[0], shard[2]
        if not any((core, oy) == group for core, _, oy in todo):
            program.append(("finish", group))
            late.append(group)
            now += 0.3
    program.append(("ship", late.pop()))
    return program, now


def kernel(features_hbm, counts, projection_hbm, taken, back, features, projection, emb, rows, cols, best, count, means, *sems):
    load, link_send, link_recv, twin_send, twin_recv, out_send, out_recv, back_send, back_recv = sems
    grp, dev = lax.axis_index("grp"), lax.axis_index("dev")
    y, c = grp // 2, grp % 2
    x, z = dev // NZ, dev % NZ
    sign = 1 - 2 * c

    def device(x, y, z, c):
        return (y * 2 + c, x * NZ + z)

    def near(dx=0, dy=0, dz=0):
        return device((x + sign * dx + NX) % NX, (y + sign * dy + NY) % NY, (z + sign * dz + NZ) % NZ, c)

    twin = device(x, y, z, 1 - c)
    special = jnp.logical_and(z == x + NX * c, x == y)

    barrier = pltpu.get_barrier_semaphore()

    def greet(target):
        pl.semaphore_signal(barrier, inc=1, device_id=target, device_id_type=MESH)

    def back_source(k):
        return jnp.logical_and(special, z == k)

    load_features = pltpu.make_async_copy(features_hbm, features, load.at[0])
    load_projection = pltpu.make_async_copy(projection_hbm, projection, load.at[1])
    load_features.start()
    load_projection.start()
    for k in range(NZ):
        @pl.when(jnp.logical_not(back_source(k)))
        def _():
            greet(device(z % NX, x, k, z // NX))

    for dx in range(NX):
        for dz in range(NZ):
            if (dx, dz) != (0, 0):
                greet(device((x + dx) % NX, y, (z + dz) % NZ, c))
    greet(near(0, 1, 0))
    greet(near(0, -1, 0))
    greet(twin)

    load_features.wait()
    load_projection.wait()

    raw = jnp.dot(features[...].reshape(2 * SLOTS, -1), projection[...], preferred_element_type=jnp.float32)
    scale = lax.rsqrt(jnp.sum(raw * raw, axis=1, keepdims=True) + 1e-06)
    embed = (raw * scale).astype(jnp.bfloat16).astype(jnp.float32)
    slot = lax.broadcasted_iota(jnp.int32, (SLOTS, 1), 0)
    for s in range(2):
        block = embed[s * SLOTS:(s + 1) * SLOTS]
        valid = slot < counts[s]
        number = jnp.where(slot == SLOTS - 1, counts[s].astype(jnp.float32), 0.0)
        rows[z, s] = jnp.where(valid, block, number).astype(jnp.bfloat16)
        emb[pl.ds(s * KEEP, KEEP), :] = jnp.where(valid, block, block[0:1])[:KEEP]
    cols[y, x, c] = emb[...].astype(jnp.bfloat16)

    pl.semaphore_wait(barrier, (NX * NZ - 1) + 3 + NZ - special.astype(jnp.int32))

    def arrived(ref, sem):
        pltpu.make_async_copy(ref, ref, sem).wait()

    def place(core, ox, oy):
        return (y + sign * oy + NY) % NY, (x + sign * ox + NX) % NX, (c if core == 0 else 1 - c)

    def piece_ref(key):
        if key[0] == "row":
            return rows.at[(z + sign * key[1] + NZ) % NZ, key[2] * QUARTER // SLOTS, pl.ds(key[2] * QUARTER % SLOTS, QUARTER)]
        _, p, ox, oy = key
        return cols.at[(*place(0, ox, oy), pl.ds(PIECES[p][1], PIECES[p][2] - PIECES[p][1]))]

    number_of = {}
    for link, keys in LINKS.items():
        for i in range(len(keys)):
            number_of[(link, i)] = len(number_of)

    def link_copy(link, i):
        ref = piece_ref(at_sender(link, LINKS[link][i]))
        index = number_of[(link, i)]
        return pltpu.make_async_remote_copy(
            src_ref=ref, dst_ref=ref, send_sem=link_send.at[index], recv_sem=link_recv.at[index], device_id=near(*link), device_id_type=MESH)

    def send_event(link, i):
        if i >= WINDOW:
            link_copy(link, i - WINDOW).wait_send()
        link_copy(link, i).start()

    def arrive_event(link, i):
        arrived(piece_ref(LINKS[link][i]), link_recv.at[number_of[(link, i)]])

    def way_ref(way, core, ox, oy):
        return cols.at[(*place(core, ox, oy), pl.ds(WAYS[way][0], WAYS[way][1] - WAYS[way][0]))]

    def to_twin_event(way, ox, oy):
        index = (way * NX + ox) * NY + oy
        ref = way_ref(way, 0, ox, oy)
        pltpu.make_async_remote_copy(
            src_ref=ref, dst_ref=ref, send_sem=twin_send, recv_sem=twin_recv.at[index], device_id=twin, device_id_type=MESH).start()

    def twin_event(way, ox, oy):
        arrived(way_ref(way, 1, ox, oy), twin_recv.at[(way * NX + -ox % NX) * NY + -oy % NY])

    counted = set()

    def count_rows(tile):
        counted.add(tile)
        ring = (z + sign * tile + NZ) % NZ
        for s in range(2):
            count[pl.ds(2 * ring + s, 1)] = rows[ring, s, pl.ds(SLOTS - 16, 16), 0:SLOTS].astype(jnp.float32)[15:16]

    def block_step(core, ox, oy, tiles):
        column, line, half = place(core, ox, oy)
        block = cols[column, line, half]
        for tile in tiles:
            if tile not in counted:
                count_rows(tile)
            ring = (z + sign * tile + NZ) % NZ
            score = lax.dot_general(block, rows[ring].reshape(2 * SLOTS, -1), (((1,), (1,)), ((), ())), preferred_element_type=jnp.float32)
            for b in range(2):
                top = jnp.max(score[b * KEEP:(b + 1) * KEEP], axis=0, keepdims=True)
                for s in range(2):
                    best[column, half, line, b, pl.ds(2 * ring + s, 1)] = top[:, s * SLOTS:(s + 1) * SLOTS]

    lane = lax.broadcasted_iota(jnp.int32, (1, SLOTS), 1)

    def group_place(core, oy):
        column, _, half = place(core, 0, oy)
        return column, half

    def out_copy(column, line, half):
        return pltpu.make_async_remote_copy(
            src_ref=best.at[column, half, line], dst_ref=taken.at[x, z], send_sem=out_send, recv_sem=out_recv,
            device_id=device(column, y, line + NX * half, c), device_id_type=MESH)

    def back_copy(column, half):
        return pltpu.make_async_remote_copy(
            src_ref=means.at[column, half], dst_ref=back.at[z], send_sem=back_send, recv_sem=back_recv,
            device_id=device(y, column, x + NX * c, half), device_id_type=MESH)

    def finish_step(core, oy):
        column, half = group_place(core, oy)
        mean = jnp.zeros((2 * NZ, SLOTS), jnp.float32)
        number = count[...]
        for line in range(NX):
            for b in range(2):
                top = jnp.where(lane < KEEP, best[column, half, line, b], 0.0)
                value = jnp.sum(top, axis=1, keepdims=True) / number
                best[column, half, line, b] = jnp.where(lane == SLOTS - 1, value, top)
                mean = jnp.where(lane == 2 * line + b, value, mean)
        means[column, half] = mean

    def ship_step(core, oy):
        column, half = group_place(core, oy)
        for line in range(NX):
            here = jnp.logical_and(column == x, line + NX * half == z)

            @pl.when(jnp.logical_not(here))
            def _():
                out_copy(column, line, half).start()

            @pl.when(here)
            def _():
                pltpu.make_async_copy(best.at[column, half, line], taken.at[x, z], out_recv).start()

        here = jnp.logical_and(special, jnp.logical_and(column == y, half == c))

        @pl.when(jnp.logical_not(here))
        def _():
            back_copy(column, half).start()

        @pl.when(here)
        def _():
            pltpu.make_async_copy(means.at[column, half], back.at[z], back_recv).start()

    handlers = {"send": send_event, "arrive": arrive_event, "to_twin": to_twin_event, "twin": twin_event,
                "block": lambda shard, tiles: block_step(*shard, tiles), "finish": lambda group: finish_step(*group), "ship": lambda group: ship_step(*group)}
    for entry in plan()[0]:
        handlers[entry[0]](*entry[1:])

    arrived(back, back_recv)
    arrived(taken, out_recv)
    for link, keys in LINKS.items():
        for i in range(max(len(keys) - WINDOW, 0), len(keys)):
            link_copy(link, i).wait_send()
    arrived(cols.at[0:NY // 2], twin_send)
    arrived(taken.at[0:NX - 1], out_send)
    arrived(taken.at[NX - 1, 0:NZ - 1], out_send)
    arrived(back.at[0:NZ - 1], back_send)

    @pl.when(jnp.logical_not(special))
    def _():
        arrived(back.at[0], back_send)


def place_kernel(taken, back, out, chamfer, turned, mean):
    lane = lax.broadcasted_iota(jnp.int32, (1, SLOTS), 1)
    for k in range(NZ):
        turned[...] = back[k].T
        for i in range(NX):
            mean[pl.ds(16 * i + 2 * k, 2), 0:16] = turned[pl.ds(2 * i, 2), :]
    for i in range(NX):
        line = jnp.zeros((16, SLOTS), jnp.float32)
        for k in range(NZ):
            for b in range(2):
                value = taken[i, k, b]
                line = jnp.where(lane == 2 * k + b, value[:, SLOTS - 1:SLOTS], line)
                out[pl.ds(16 * i, 16), 2 * k + b, :] = jnp.where(lane < KEEP, value, 0.0)
        part = pl.ds(16 * i, 16)
        mean[part, 0:16] = 0.5 * (mean[part, 0:16] + line[:, 0:16])
    chamfer[...] = mean[:, 0:16].T


def on_device(features, tile_counts, projection):
    dma = pltpu.SemaphoreType.DMA
    width = projection.shape[1]
    vmem = pl.BlockSpec(memory_space=pltpu.VMEM)
    anywhere = pl.BlockSpec(memory_space=pl.ANY)
    sends = sum(len(keys) for keys in LINKS.values())
    f32 = jnp.float32
    taken, back = pl.pallas_call(
        kernel,
        name="compare",
        out_shape=(jax.ShapeDtypeStruct((NX, NZ, 2, 16, SLOTS), f32), jax.ShapeDtypeStruct((NZ, 16, SLOTS), f32)),
        in_specs=[anywhere, pl.BlockSpec(memory_space=pltpu.SMEM), anywhere],
        out_specs=(vmem, vmem),
        scratch_shapes=[
            pltpu.VMEM(features.shape, jnp.bfloat16),
            pltpu.VMEM(projection.shape, jnp.bfloat16),
            pltpu.VMEM((SHARD, width), f32),
            pltpu.VMEM((NZ, 2, SLOTS, width), jnp.bfloat16),
            pltpu.VMEM((NY, NX, 2, SHARD, width), jnp.bfloat16),
            pltpu.VMEM((NY, 2, NX, 2, 16, SLOTS), f32),
            pltpu.VMEM((16, SLOTS), f32),
            pltpu.VMEM((NY, 2, 16, SLOTS), f32),
            dma((2,)), dma((sends,)), dma((sends,)), dma, dma((32,)), dma, dma, dma, dma,
        ],
        compiler_params=pltpu.CompilerParams(collective_id=0, has_side_effects=True, vmem_limit_bytes=56 * 2**20),
    )(features, tile_counts, projection)
    out, chamfer = pl.pallas_call(
        place_kernel,
        name="place",
        out_shape=(jax.ShapeDtypeStruct((64, 16, SLOTS), f32), jax.ShapeDtypeStruct((16, 64), f32)),
        in_specs=[vmem, vmem],
        out_specs=(vmem, vmem),
        scratch_shapes=[pltpu.VMEM((SLOTS, 16), f32), pltpu.VMEM((64, SLOTS), f32)],
    )(taken, back)
    return out, chamfer.T


def solution(mesh):
    return jax.shard_map(
        on_device,
        mesh=mesh,
        in_specs=(P(("grp", "dev"), None, None), P(("grp", "dev")), P()),
        out_specs=(P("grp", "dev", None), P("grp", "dev")),
        check_vma=False,
    )
```

time: 71.7 us -> 62.8 us (0.88)
  Pallas kernels: 69.4 us -> 62 us
  local copies, waits for them, and re-layouts: 1.43 us -> 0 us
    pallas_call x1, Pallas kernels: 67.1 us -> 59.8 us  [on_device(): pl.pallas_call(kernel, name='compare', out_shape=(jax.ShapeDtypeStruct((N...]
    pallas_call x1 -> x0, local copies, waits for them, and re-layouts: 1.43 us -> none  [on_device(): pl.pallas_call(place_kernel, name='place', out_shape=(jax.ShapeDtypeStruc...]
where the time goes in v3:
time: 62.8 us; the launch traced here: 62.6 us
  Pallas kernels  62 us (99%)
  between operations  0.64 us (1%)
    pallas_call x1, Pallas kernels, on_device(): pl.pallas_call(kernel, name='compare', out_shape=(jax.ShapeDtypeStruct((N...  59.8 us
    pallas_call x1, Pallas kernels, on_device(): pl.pallas_call(place_kernel, name='place', out_shape=(jax.ShapeDtypeStruc...  2.19 us

profile of v3, /device:TPU:5, one launch (start us, length us, event | category | flops | bytes accessed | tf_op | source)
XLA Modules:
  0.0 62.6 jit_solution(9498781242508372567)
XLA Ops:
  0.6 59.8 %compare.1 = (f32[4,8,2,16,128]{4,3,2,1,0:T(8,128)}, f32[8,16,128]{2,1,0:T(8,128)}) custom-call(bf16[2,128,768]{2,1,0:T(8,128)(2,1)} %features_hbm.1, s32[2]{0:T(128)} %counts.1, bf16[768,512]{1,0:T(8,128)(2,1)} %projection_hbm.1), custom_call_target="tpu_custom_call" | custom-call | tf_op jit(solution)/shard_map/compare/pallas_call | solution.py:362
  60.5 2.2 %place.1 = (f32[64,16,128]{2,1,0:T(8,128)}, f32[16,64]{1,0:T(8,128)}) custom-call(f32[4,8,2,16,128]{4,3,2,1,0:T(8,128)} %get-tuple-element.6.taken, f32[8,16,128]{2,1,0:T(8,128)} %get-tuple-element.7.back), custom_call_target="tpu_custom_call" | custom-call | tf_op jit(solution)/shard_map/place/pallas_call | solution.py:381

commit v4 on v3

--- a/solution.py
+++ b/solution.py
@@ -16,9 +16,9 @@
 QUARTER = 128
 WINDOW = 2
 
-T_ROW = 0.0213
-T_HOP = 2.5
-T_TWIN = 2.2
+T_ROW = 0.019
+T_HOP = 2.2
+T_TWIN = 2.0
 T_TILE, T_BLOCK, T_EVENT = 0.07, 0.1, 0.02
 MOST = 4
 

time: 62.8 us -> 62.5 us (level)
  no operation moved by 1% of the time
where the time goes in v4:
time: 62.5 us; the launch traced here: 62.3 us
  Pallas kernels  61.7 us (99%)
  between operations  0.64 us (1%)
    pallas_call x1, Pallas kernels, on_device(): pl.pallas_call(kernel, name='compare', out_shape=(jax.ShapeDtypeStruct((N...  59.5 us
    pallas_call x1, Pallas kernels, on_device(): pl.pallas_call(place_kernel, name='place', out_shape=(jax.ShapeDtypeStruc...  2.19 us

profile of v4, /device:TPU:5, one launch (start us, length us, event | category | flops | bytes accessed | tf_op | source)
XLA Modules:
  0.0 62.3 jit_solution(9925423354432403104)
XLA Ops:
  0.6 59.5 %compare.1 = (f32[4,8,2,16,128]{4,3,2,1,0:T(8,128)}, f32[8,16,128]{2,1,0:T(8,128)}) custom-call(bf16[2,128,768]{2,1,0:T(8,128)(2,1)} %features_hbm.1, s32[2]{0:T(128)} %counts.1, bf16[768,512]{1,0:T(8,128)(2,1)} %projection_hbm.1), custom_call_target="tpu_custom_call" | custom-call | tf_op jit(solution)/shard_map/compare/pallas_call | solution.py:362
  60.1 2.2 %place.1 = (f32[64,16,128]{2,1,0:T(8,128)}, f32[16,64]{1,0:T(8,128)}) custom-call(f32[4,8,2,16,128]{4,3,2,1,0:T(8,128)} %get-tuple-element.6.taken, f32[8,16,128]{2,1,0:T(8,128)} %get-tuple-element.7.back), custom_call_target="tpu_custom_call" | custom-call | tf_op jit(solution)/shard_map/place/pallas_call | solution.py:381
